TPU v7x, 32 devices: a whole 2x2x4 slice. The times are simulated.
32 devices in a mesh: tm: 8 (over y, x, core), col: 4 (over z).
Axes of the slice: x: 2, y: 2, z: 4, core: 2. Of those that a mesh axis runs over, the one named last changes fastest.
Arguments:
- init_mean: float32 [256], replicated, may hold values from -5 to 5
- drive: float32 [2048, 256], P('tm'), may hold values from -0.24 to 0.24
- decay: float32 [2048, 256], P('tm'), may hold values from 0 to 1
- transition_raw: float32 [256, 256], replicated, may hold values from -1 to 2
- in_weight: bfloat16 [256, 1024], replicated, may hold values from -0.375 to 0.375
- in_bias: float32 [1024], replicated, may hold values from -3 to 3
- out_weight: bfloat16 [1024, 8192], P(None, 'col'), may hold values from -0.0625 to 0.0625
- rate_grad: bfloat16 [2048, 8192], P('tm', 'col'), may hold values from -0.23925781 to 0.23925781
Outputs:
- means: float32 [2048, 256], P('tm', 'col')
- adjoints: float32 [2048, 256], P('tm', 'col')
All inputs are finite; a program needn't handle non-finite values.
Results may differ from a plain program's by a relative error of at most 0.0036.
Values sent between devices are 32-bit elements; how exact they have to be, the bound alone decides.
A program may use at most 128 MiB of HBM per device.

v0:
```python
import jax
import jax.numpy as jnp
from jax import lax
from jax.sharding import PartitionSpec as P

HIGHEST = lax.Precision.HIGHEST


def from_behind(value, axis, by):
    length = lax.axis_size(axis)
    pairs = [(i, i + by) for i in range(length) if 0 <= i + by < length]
    return lax.ppermute(value, axis, pairs)


def orthogonal(matrix):
    factor = matrix
    for sweep in range(12):
        factor = 1.5 * factor - 0.5 * jnp.dot(
            factor, jnp.dot(factor.T, factor, precision=HIGHEST), precision=HIGHEST
        )
    return factor


def local(init_mean, drive, decay, transition_raw, in_weight, in_bias, out_weight, rate_grad):
    rotation = orthogonal(transition_raw)
    rotation_t = rotation.T
    latent = rotation.shape[0]
    col_width = latent // lax.axis_size("col")
    col_start = lax.axis_index("col") * col_width
    hidden_grad = lax.psum(
        lax.dot_general(
            rate_grad, out_weight, (((1,), (1,)), ((), ())), preferred_element_type=jnp.float32
        ),
        "col",
    )
    row_ids = lax.broadcasted_iota(jnp.int32, (col_width, latent), 0)
    col_ids = lax.broadcasted_iota(jnp.int32, (col_width, latent), 1)
    initial = jnp.where(col_ids == row_ids + col_start, 1.0, 0.0).astype(jnp.float32)
    zero_vec = jnp.zeros((latent,), jnp.float32)

    def forward_step(carried, inputs):
        basis_now, offset_now = carried
        keep_rate, drive_row = inputs
        basis_next = jnp.dot(basis_now, rotation_t, precision=HIGHEST) * keep_rate[None, :]
        offset_next = jnp.dot(offset_now, rotation_t, precision=HIGHEST) * keep_rate + drive_row
        return ((basis_next, offset_next), (basis_next, offset_next))

    (element_rows, offset), (history, offset_history) = lax.scan(
        forward_step, (initial, zero_vec), (decay, drive), unroll=8
    )
    element = lax.all_gather(element_rows, "col", axis=0, tiled=True)
    slab_index = lax.axis_index("tm")

    def relay_forward(counter, incoming):
        outgoing = jnp.dot(incoming, element, precision=HIGHEST) + offset
        received = from_behind(outgoing, "tm", 1)
        return jnp.where(slab_index == 0, init_mean, received)

    incoming = lax.fori_loop(0, lax.axis_size("tm") - 1, relay_forward, init_mean)
    own_part = lax.dynamic_slice_in_dim(incoming, col_start, col_width)
    partial_value = jnp.einsum("tjs,j->ts", history, own_part, precision=HIGHEST)
    means_full = lax.psum(partial_value, "col") + offset_history
    means_low = means_full.astype(jnp.bfloat16)
    preact = jnp.dot(means_low, in_weight, preferred_element_type=jnp.float32) + in_bias
    hidden = jnp.tanh(preact)
    pre_grad = (hidden_grad * (1.0 - hidden * hidden)).astype(jnp.bfloat16)
    state_grad = lax.dot_general(
        pre_grad, in_weight, (((1,), (1,)), ((), ())), preferred_element_type=jnp.float32
    )

    def local_back(carried, inputs):
        keep_rate, grad_row = inputs
        adjoint = carried + grad_row
        return (jnp.dot(adjoint * keep_rate, rotation, precision=HIGHEST), adjoint)

    local_adj, back_history = lax.scan(
        local_back, zero_vec, (decay, state_grad), reverse=True, unroll=8
    )

    def relay_backward(counter, after_adj):
        outgoing = jnp.dot(element, after_adj, precision=HIGHEST) + local_adj
        return from_behind(outgoing, "tm", -1)

    after_adj = lax.fori_loop(0, lax.axis_size("tm") - 1, relay_backward, zero_vec)

    def basis_step(carried, keep_rate):
        return (jnp.dot(carried * keep_rate[None, :], rotation, precision=HIGHEST), carried)

    unused_end, basis_history = lax.scan(basis_step, initial, decay, reverse=True, unroll=8)
    own_after = lax.dynamic_slice_in_dim(after_adj, col_start, col_width)
    adjoint_terms = jnp.einsum("tjs,j->ts", basis_history, own_after, precision=HIGHEST)
    adjoints_full = lax.psum(adjoint_terms, "col") + back_history
    means_out = lax.dynamic_slice_in_dim(means_full, col_start, col_width, 1)
    adjoints_out = lax.dynamic_slice_in_dim(adjoints_full, col_start, col_width, 1)
    return (means_out, adjoints_out)


def solution(mesh):
    return jax.shard_map(
        local,
        mesh=mesh,
        in_specs=(P(), P("tm", None), P("tm", None), P(), P(), P(), P(None, "col"), P("tm", "col")),
        out_specs=(P("tm", "col"), P("tm", "col")),
        check_vma=False,
    )
```

profile of v0, /device:TPU:0, one launch (start us, length us, event | category | flops | bytes accessed | tf_op | source)
XLA Modules:
  0.0 630.8 jit_solution(16460690562373309950)
XLA Ops:
  8.4 1.7 fusion.82
  10.1 1.5 fusion.43
  23.0 8.1 %broadcast.17.clone = f32[32,8,64,256]{3,2,1,0:T(8,128)} broadcast(f32[]{:T(128)} %constant.120.clone.1), dimensions={} | broadcast | bytes 16777220 | tf_op jit(solution)/shard_map/broadcast.5
  31.1 196.2 %while.75 = (s32[]{:T(128)}, f32[64,256]{1,0:T(8,128)S(1)}, f32[256]{0:T(256)S(1)}, f32[32,8,64,256]{3,2,1,0:T(8,128)}, f32[32,8,256]{2,1,0:T(8,128)S(1)}, /*ind...) while((s32[]{:T(128)}, f32[64,256]{1,0:T(8,128)S(1)}, ...), condition=%wide.region_1.2_spmd.clone, body=%wide.region_0.0_spmd.clone.sunk | while | flops 409080064 | bytes 6941471 | solution.py:48
  220.9 1.5 constant_dynamic-slice_fusion.46
  227.3 15.6 %all_gather.3 = f32[256,256]{1,0:T(8,128)S(1)} all-gather(f32[64,256]{1,0:T(8,128)S(1)} %get-tuple-element.368), channel_id=1, replica_groups=mesh['tm'=8,'col'=4] {'col'}, dimensions={0}, use_global_device_ids=true | all-gather | bytes 327680 | tf_op jit(solution)/shard_map/all_gather | solution.py:51
  242.9 33.0 %while.71 = (s32[]{:T(128)}, f32[256]{0:T(256)S(1)}, pred[]{:T(512)}, f32[256,256]{1,0:T(8,128)S(1)}, f32[256]{0:T(256)S(1)}, /*index=5*/f32[256]{0:T(256)S(1)}, s32[]{:T(128)}) while((s32[]{:T(128)}, f32[256]{0:T(256)S(1)}, pred[]{:T(512)}, f32[256,256]{1,0:T(8,128)S(1)}, f32[256]{0:T(256)S(1)}, /*index=5*/f32[256]{0:T(256)S(1)}, ...), condition=%wide.region_3.4_spmd, body=%wide.region_2.3_spmd.sunk | while | flops 786946 | bytes 274550 | solution.py:59
  245.4 4.1 collective-permute-start
  250.5 4.1 collective-permute-start
  255.6 4.1 collective-permute-start
  260.7 4.1 collective-permute-start
  265.9 4.1 collective-permute-start
  271.0 4.1 collective-permute-start
  275.9 11.4 %fusion.51 = f32[1,256,256]{2,0,1:T(1,128)S(1)} fusion(f32[256,64,256]{2,1,0:T(8,128)} %bitcast.618, f32[256]{0:T(256)S(1)} %get-tuple-element.370, s32[]{:T(128)S(6)} %select_n.23), kind=kOutput, calls=%fused_computation.147 | convolution fusion | flops 50331648 | bytes 17039876 | tf_op jit(solution)/shard_map/tjs,j->ts/dot_general | solution.py:61
  288.1 2.2 fusion.94
  290.8 7.9 %broadcast.17.clone.1 = f32[32,8,64,256]{3,2,1,0:T(8,128)} broadcast(f32[]{:T(128)} %constant.120.clone.1), dimensions={} | broadcast | bytes 16777220 | tf_op jit(solution)/shard_map/broadcast.5
  298.7 127.6 %while.72 = (s32[]{:T(128)}, f32[64,256]{1,0:T(8,128)S(1)}, f32[32,8,64,256]{3,2,1,0:T(8,128)}, f32[32,8,256]{2,1,0:T(8,128)}, f32[256,256]{1,0:T(8,128)S(1)}, /...) while((s32[]{:T(128)}, f32[64,256]{1,0:T(8,128)S(1)}, ...), condition=%wide.region_6.7_spmd, body=%wide.region_5.6_spmd.sunk | while | flops 402784256 | bytes 5202193 | solution.py:89
  427.3 1.8 fusion.30
  429.1 94.4 %while.73 = (s32[]{:T(128)}, f32[256]{0:T(256)S(1)}, f32[32,8,256]{2,1,0:T(8,128)S(1)}, f32[32,8,256]{2,1,0:T(8,128)S(1)}, f32[32,8,256]{2,1,0:T(8,128)}, /*inde...) while((s32[]{:T(128)}, f32[256]{0:T(256)S(1)}, ...), condition=%wide.region_9.10_spmd, body=%wide.region_8.9_spmd.sunk | while | flops 6295562 | bytes 2220313 | solution.py:76
  523.5 43.4 %while.74 = (s32[]{:T(128)}, f32[256]{0:T(256)S(1)}, f32[256,256]{1,0:T(8,128)S(1)}, f32[256]{0:T(256)S(1)}, s32[]{:T(128)}) while((s32[]{:T(128)}, f32[256]{0:T(256)S(1)}, f32[256,256]{1,0:T(8,128)S(1)}, f32[256]{0:T(256)S(1)}, s32[]{:T(128)}) %tuple.252), condition=%wide.region_11.12_spmd, body=%wide.region_10.11_spmd.sunk | while | flops 786690 | bytes 271461 | solution.py:84
  523.8 1.3 collective-permute-start.1
  525.1 4.2 collective-permute-done.1
  529.6 1.3 collective-permute-start.1
  530.9 5.0 collective-permute-done.1
  536.2 1.3 collective-permute-start.1
  537.6 4.3 collective-permute-done.1
  543.5 5.0 collective-permute-done.1
  550.2 4.5 collective-permute-done.1
  556.3 4.5 collective-permute-done.1
  562.4 4.5 collective-permute-done.1
  566.9 11.3 %fusion.49 = f32[1,256,256]{2,0,1:T(1,128)S(1)} fusion(f32[256,64,256]{2,1,0:T(8,128)} %bitcast.619, f32[256]{0:T(256)S(1)} %get-tuple-element.374, s32[]{:T(128)S(6)} %select_n.23), kind=kOutput, calls=%fused_computation.145 | convolution fusion | flops 50331648 | bytes 17039876 | tf_op jit(solution)/shard_map/tjs,j->ts/dot_general | solution.py:91
  579.8 42.4 %all-reduce.4.cloned.1.call-done = f32[256,256]{1,0:T(8,128)} async-done(((f32[256,256]{1,0:T(8,128)}), f32[256,256]{1,0:T(8,128)}) %all-reduce.4.cloned.1.call-update) | async-done | bytes 262160 | tf_op jit(solution)/shard_map/psum | solution.py:92
  (2181 shorter events, 426.2 us)
Async XLA Ops:
  7.2 280.9 %copy-start = (bf16[256,2048]{1,0:T(8,128)(2,1)S(1)}, bf16[256,2048]{1,0:T(8,128)(2,1)}, u32[]{:S(2)}) copy-start(bf16[256,2048]{1,0:T(8,128)(2,1)} %param.25) | copy-start | bytes 3145732
  7.2 419.1 %all-reduce.6.cloned.1.call-start = ((), (), s32[]{:S(2)}) async-start(), calls=%async_computation.1 | async-start | bytes 2621440 | tf_op jit(solution)/shard_map/psum | solution.py:62
  31.1 211.8 %copy-start.2 = (f32[256]{0:T(256)S(1)}, f32[256]{0:T(256)}, u32[]{:S(2)}) copy-start(f32[256]{0:T(256)} %param.18) | copy-start | bytes 3076
  243.1 2.1 collective-permute-start
  245.4 4.9 collective-permute-start
  250.5 4.9 collective-permute-start
  255.6 4.9 collective-permute-start
  260.7 4.9 collective-permute-start
  265.9 4.9 collective-permute-start
  271.0 4.9 collective-permute-start
  275.9 12.2 %copy-start.4 = (bf16[1024,2048]{1,0:T(8,128)(2,1)S(1)}, bf16[1024,2048]{1,0:T(8,128)(2,1)}, u32[]{:S(2)}) copy-start(bf16[1024,2048]{1,0:T(8,128)(2,1)} %param.24) | copy-start | bytes 12582916
  290.4 331.8 %all-reduce.4.cloned.1.call-start = ((), (), s32[]{:S(2)}) async-start(), calls=%async_computation | async-start | bytes 524288 | tf_op jit(solution)/shard_map/psum | solution.py:92
  298.6 128.6 %copy-start.1 = (bf16[256,1024]{1,0:T(8,128)(2,1)S(1)}, bf16[256,1024]{1,0:T(8,128)(2,1)}, u32[]{:S(2)}) copy-start(bf16[256,1024]{1,0:T(8,128)(2,1)} %param.22) | copy-start | bytes 1572868
  298.6 128.6 %copy-start.3 = (f32[1024]{0:T(1024)S(1)}, f32[1024]{0:T(1024)}, u32[]{:S(2)}) copy-start(f32[1024]{0:T(1024)} %param.23) | copy-start | bytes 12292
  523.8 5.5 collective-permute-start.1
  529.6 6.4 %collective-permute-start.1 = (f32[256]{0:T(256)S(1)}, f32[256]{0:T(256)S(1)}, u32[]{:S(2)}, u32[]{:S(2)}) collective-permute-start(f32[256]{0:T(256)S(1)} %add.341), channel_id=1, source_target_pairs={{4,0},{8,4},{12,8},{16,12},{20,16},{24,20},{28,24},{5,1},{9,5},{13... | collective-permute-start | bytes 3080 | tf_op jit(solution)/shard_map/while/body/eval_jaxpr/ppermute | solution.py:12
  536.2 5.7 collective-permute-start.1
  542.2 6.4 %collective-permute-start.1 = (f32[256]{0:T(256)S(1)}, f32[256]{0:T(256)S(1)}, u32[]{:S(2)}, u32[]{:S(2)}) collective-permute-start(f32[256]{0:T(256)S(1)} %add.341), channel_id=1, source_target_pairs={{4,0},{8,4},{12,8},{16,12},{20,16},{24,20},{28,24},{5,1},{9,5},{13... | collective-permute-start | bytes 3080 | tf_op jit(solution)/shard_map/while/body/eval_jaxpr/ppermute | solution.py:12
  548.9 5.8 collective-permute-start.1
  555.0 5.8 collective-permute-start.1
  561.1 5.8 collective-permute-start.1
Sparse Core Ops, SparseCore 0:
  290.5 70.0 all-reduce.5
  579.1 43.0 all-reduce.3
where the time goes:
time: 638 us; the launch traced here: 631 us
  matrix products  269 us (42%)
  local copies, waits for them, and re-layouts  185 us (29%)
  waiting for transfers between devices  80.1 us (13%)
  starting transfers between devices  35.6 us (6%)
  loops' own time  24.2 us (4%)
  blocking collectives  15.6 us (2%)
  between operations  14.4 us (2%)
  other arithmetic  7.1 us (1%)
    dot_general x256, matrix products, forward_step(): jnp.dot(basis_now, rotation_t, precision=HIGHEST) * keep_rate[None, :]  63.9 us
    dot_general x256, matrix products, basis_step(): jnp.dot(carried * keep_rate[None, :], rotation, precision=HIGHEST)  62.1 us
    dynamic_update_slice x128, local copies, waits for them, and re-layouts, local(): lax.scan(forward_step, (initial, zero_vec), (decay, drive), unroll=8)  54.9 us
    dot_general x256, matrix products, forward_step(): jnp.dot(offset_now, rotation_t, precision=HIGHEST) * keep_rate + drive_row  49.3 us
    dot_general x256, matrix products, local_back(): return (jnp.dot(adjoint * keep_rate, rotation, precision=HIGHEST), adjoint)  49.1 us
    psum x1, waiting for transfers between devices, local(): adjoints_full = lax.psum(adjoint_terms, 'col') + back_history  42.4 us
    slice x32, local copies, waits for them, and re-layouts, local(): lax.scan(forward_step, (initial, zero_vec), (decay, drive), unroll=8)  40.5 us
    ppermute x14, waiting for transfers between devices, from_behind(): return lax.ppermute(value, axis, pairs)  37.6 us
  transfers between devices with their start and end apart: 16, of which 15 were waited for; matrix products, arithmetic and copies ran while one was open for 21% of the time, Pallas kernels for 0%

commit v1 on v0

--- a/solution.py
+++ b/solution.py
@@ -89,7 +89,7 @@
     unused_end, basis_history = lax.scan(basis_step, initial, decay, reverse=True, unroll=8)
     own_after = lax.dynamic_slice_in_dim(after_adj, col_start, col_width)
     adjoint_terms = jnp.einsum("tjs,j->ts", basis_history, own_after, precision=HIGHEST)
-    adjoints_full = lax.psum(adjoint_terms, "col") + back_history
+    adjoints_full = jnp.sum(lax.all_gather(adjoint_terms, "col"), axis=0) + back_history
     means_out = lax.dynamic_slice_in_dim(means_full, col_start, col_width, 1)
     adjoints_out = lax.dynamic_slice_in_dim(adjoints_full, col_start, col_width, 1)
     return (means_out, adjoints_out)

time: 638 us -> 631 us (0.989)
  waiting for transfers between devices: 80.1 us -> 72.7 us
    psum x1 -> x0, waiting for transfers between devices: 42.4 us -> none  [local(): adjoints_full = lax.psum(adjoint_terms, 'col') + back_history]
    all_gather x0 -> x1, waiting for transfers between devices: none -> 35 us  [local(): lax.all_gather(adjoint_terms, 'col')]
where the time goes in v1:
time: 631 us; the launch traced here: 624 us
  matrix products  269 us (43%)
  local copies, waits for them, and re-layouts  185 us (29%)
  waiting for transfers between devices  72.7 us (12%)
  starting transfers between devices  35.6 us (6%)
  loops' own time  24.2 us (4%)
  blocking collectives  15.6 us (2%)
  between operations  14.4 us (2%)
  other arithmetic  7.52 us (1%)
    dot_general x256, matrix products, forward_step(): jnp.dot(basis_now, rotation_t, precision=HIGHEST) * keep_rate[None, :]  63.9 us
    dot_general x256, matrix products, basis_step(): jnp.dot(carried * keep_rate[None, :], rotation, precision=HIGHEST)  62.1 us
    dynamic_update_slice x128, local copies, waits for them, and re-layouts, local(): lax.scan(forward_step, (initial, zero_vec), (decay, drive), unroll=8)  54.9 us
    dot_general x256, matrix products, forward_step(): jnp.dot(offset_now, rotation_t, precision=HIGHEST) * keep_rate + drive_row  49.3 us
    dot_general x256, matrix products, local_back(): return (jnp.dot(adjoint * keep_rate, rotation, precision=HIGHEST), adjoint)  49.1 us
    slice x32, local copies, waits for them, and re-layouts, local(): lax.scan(forward_step, (initial, zero_vec), (decay, drive), unroll=8)  40.5 us
    ppermute x14, waiting for transfers between devices, from_behind(): return lax.ppermute(value, axis, pairs)  37.6 us
    ppermute x14, starting transfers between devices, from_behind(): return lax.ppermute(value, axis, pairs)  35.3 us
  transfers between devices with their start and end apart: 16, of which 15 were waited for; matrix products, arithmetic and copies ran while one was open for 21% of the time, Pallas kernels for 0%

profile of v1, /device:TPU:0, one launch (start us, length us, event | category | flops | bytes accessed | tf_op | source)
XLA Modules:
  0.0 623.8 jit_solution(4177611573017093392)
XLA Ops:
  8.4 1.7 fusion.82
  10.1 1.5 fusion.43
  23.0 8.1 %broadcast.17.clone = f32[32,8,64,256]{3,2,1,0:T(8,128)} broadcast(f32[]{:T(128)} %constant.120.clone.1), dimensions={} | broadcast | bytes 16777220 | tf_op jit(solution)/shard_map/broadcast.5
  31.1 196.2 %while.75 = (s32[]{:T(128)}, f32[64,256]{1,0:T(8,128)S(1)}, f32[256]{0:T(256)S(1)}, f32[32,8,64,256]{3,2,1,0:T(8,128)}, f32[32,8,256]{2,1,0:T(8,128)S(1)}, /*ind...) while((s32[]{:T(128)}, f32[64,256]{1,0:T(8,128)S(1)}, ...), condition=%wide.region_1.2_spmd.clone, body=%wide.region_0.0_spmd.clone.sunk | while | flops 409080064 | bytes 6941471 | solution.py:48
  220.9 1.5 constant_dynamic-slice_fusion.46
  227.3 15.6 %all_gather.9 = f32[256,256]{1,0:T(8,128)S(1)} all-gather(f32[64,256]{1,0:T(8,128)S(1)} %get-tuple-element.368), channel_id=1, replica_groups=mesh['tm'=8,'col'=4] {'col'}, dimensions={0}, use_global_device_ids=true | all-gather | bytes 327680 | tf_op jit(solution)/shard_map/all_gather | solution.py:51
  242.9 33.0 %while.71 = (s32[]{:T(128)}, f32[256]{0:T(256)S(1)}, pred[]{:T(512)}, f32[256,256]{1,0:T(8,128)S(1)}, f32[256]{0:T(256)S(1)}, /*index=5*/f32[256]{0:T(256)S(1)}, s32[]{:T(128)}) while((s32[]{:T(128)}, f32[256]{0:T(256)S(1)}, pred[]{:T(512)}, f32[256,256]{1,0:T(8,128)S(1)}, f32[256]{0:T(256)S(1)}, /*index=5*/f32[256]{0:T(256)S(1)}, ...), condition=%wide.region_3.4_spmd, body=%wide.region_2.3_spmd.sunk | while | flops 786946 | bytes 274550 | solution.py:59
  245.4 4.1 collective-permute-start
  250.5 4.1 collective-permute-start
  255.6 4.1 collective-permute-start
  260.7 4.1 collective-permute-start
  265.9 4.1 collective-permute-start
  271.0 4.1 collective-permute-start
  275.9 11.4 %fusion.51 = f32[1,256,256]{2,0,1:T(1,128)S(1)} fusion(f32[256,64,256]{2,1,0:T(8,128)} %bitcast.619, f32[256]{0:T(256)S(1)} %get-tuple-element.370, s32[]{:T(128)S(6)} %select_n.23), kind=kOutput, calls=%fused_computation.147 | convolution fusion | flops 50331648 | bytes 17039876 | tf_op jit(solution)/shard_map/tjs,j->ts/dot_general | solution.py:61
  288.1 2.2 fusion.94
  290.8 7.9 %broadcast.17.clone.1 = f32[32,8,64,256]{3,2,1,0:T(8,128)} broadcast(f32[]{:T(128)} %constant.120.clone.1), dimensions={} | broadcast | bytes 16777220 | tf_op jit(solution)/shard_map/broadcast.5
  298.7 127.6 %while.72 = (s32[]{:T(128)}, f32[64,256]{1,0:T(8,128)S(1)}, f32[32,8,64,256]{3,2,1,0:T(8,128)}, f32[32,8,256]{2,1,0:T(8,128)}, f32[256,256]{1,0:T(8,128)S(1)}, /...) while((s32[]{:T(128)}, f32[64,256]{1,0:T(8,128)S(1)}, ...), condition=%wide.region_6.7_spmd, body=%wide.region_5.6_spmd.sunk | while | flops 402784256 | bytes 5202193 | solution.py:89
  427.3 1.8 fusion.30
  429.1 94.4 %while.73 = (s32[]{:T(128)}, f32[256]{0:T(256)S(1)}, f32[32,8,256]{2,1,0:T(8,128)S(1)}, f32[32,8,256]{2,1,0:T(8,128)S(1)}, f32[32,8,256]{2,1,0:T(8,128)}, /*inde...) while((s32[]{:T(128)}, f32[256]{0:T(256)S(1)}, ...), condition=%wide.region_9.10_spmd, body=%wide.region_8.9_spmd.sunk | while | flops 6295562 | bytes 2220313 | solution.py:76
  523.5 43.4 %while.74 = (s32[]{:T(128)}, f32[256]{0:T(256)S(1)}, f32[256,256]{1,0:T(8,128)S(1)}, f32[256]{0:T(256)S(1)}, s32[]{:T(128)}) while((s32[]{:T(128)}, f32[256]{0:T(256)S(1)}, f32[256,256]{1,0:T(8,128)S(1)}, f32[256]{0:T(256)S(1)}, s32[]{:T(128)}) %tuple.255), condition=%wide.region_11.12_spmd, body=%wide.region_10.11_spmd.sunk | while | flops 786690 | bytes 271461 | solution.py:84
  523.8 1.3 collective-permute-start.1
  525.1 4.2 collective-permute-done.1
  529.6 1.3 collective-permute-start.1
  530.9 5.0 collective-permute-done.1
  536.2 1.3 collective-permute-start.1
  537.6 4.3 collective-permute-done.1
  543.5 5.0 collective-permute-done.1
  550.2 4.5 collective-permute-done.1
  556.3 4.5 collective-permute-done.1
  562.4 4.5 collective-permute-done.1
  566.9 11.3 %fusion.49 = f32[1,256,256]{2,0,1:T(1,128)S(1)} fusion(f32[256,64,256]{2,1,0:T(8,128)} %bitcast.620, f32[256]{0:T(256)S(1)} %get-tuple-element.374, s32[]{:T(128)S(6)} %select_n.23), kind=kOutput, calls=%fused_computation.145 | convolution fusion | flops 50331648 | bytes 17039876 | tf_op jit(solution)/shard_map/tjs,j->ts/dot_general | solution.py:91
  579.8 35.0 %all-gather.3.cloned.1.call-done = f32[1024,256]{1,0:T(8,128)} async-done(((f32[256,256]{1,0:T(8,128)}), f32[1024,256]{1,0:T(8,128)}) %all-gather.3.cloned.1.call-update) | async-done | bytes 1048592 | tf_op jit(solution)/shard_map/all_gather | solution.py:92
  (2182 shorter events, 426.6 us)
Async XLA Ops:
  7.2 280.9 %copy-start = (bf16[256,2048]{1,0:T(8,128)(2,1)S(1)}, bf16[256,2048]{1,0:T(8,128)(2,1)}, u32[]{:S(2)}) copy-start(bf16[256,2048]{1,0:T(8,128)(2,1)} %param.25) | copy-start | bytes 3145732
  7.2 419.1 %all-reduce.3.cloned.1.call-start = ((), (), s32[]{:S(2)}) async-start(), calls=%async_computation.1 | async-start | bytes 2621440 | tf_op jit(solution)/shard_map/psum | solution.py:62
  31.1 211.8 %copy-start.2 = (f32[256]{0:T(256)S(1)}, f32[256]{0:T(256)}, u32[]{:S(2)}) copy-start(f32[256]{0:T(256)} %param.18) | copy-start | bytes 3076
  243.1 2.1 collective-permute-start
  245.4 4.9 collective-permute-start
  250.5 4.9 collective-permute-start
  255.6 4.9 collective-permute-start
  260.7 4.9 collective-permute-start
  265.9 4.9 collective-permute-start
  271.0 4.9 collective-permute-start
  275.9 12.2 %copy-start.4 = (bf16[1024,2048]{1,0:T(8,128)(2,1)S(1)}, bf16[1024,2048]{1,0:T(8,128)(2,1)}, u32[]{:S(2)}) copy-start(bf16[1024,2048]{1,0:T(8,128)(2,1)} %param.24) | copy-start | bytes 12582916
  290.4 324.5 %all-gather.3.cloned.1.call-start = ((), (), s32[]{:S(2)}) async-start(), calls=%async_computation | async-start | bytes 1310720 | tf_op jit(solution)/shard_map/all_gather | solution.py:92
  298.6 128.6 %copy-start.1 = (bf16[256,1024]{1,0:T(8,128)(2,1)S(1)}, bf16[256,1024]{1,0:T(8,128)(2,1)}, u32[]{:S(2)}) copy-start(bf16[256,1024]{1,0:T(8,128)(2,1)} %param.22) | copy-start | bytes 1572868
  298.6 128.6 %copy-start.3 = (f32[1024]{0:T(1024)S(1)}, f32[1024]{0:T(1024)}, u32[]{:S(2)}) copy-start(f32[1024]{0:T(1024)} %param.23) | copy-start | bytes 12292
  523.8 5.5 collective-permute-start.1
  529.6 6.4 %collective-permute-start.1 = (f32[256]{0:T(256)S(1)}, f32[256]{0:T(256)S(1)}, u32[]{:S(2)}, u32[]{:S(2)}) collective-permute-start(f32[256]{0:T(256)S(1)} %add.339), channel_id=1, source_target_pairs={{4,0},{8,4},{12,8},{16,12},{20,16},{24,20},{28,24},{5,1},{9,5},{13... | collective-permute-start | bytes 3080 | tf_op jit(solution)/shard_map/while/body/eval_jaxpr/ppermute | solution.py:12
  536.2 5.7 collective-permute-start.1
  542.2 6.4 %collective-permute-start.1 = (f32[256]{0:T(256)S(1)}, f32[256]{0:T(256)S(1)}, u32[]{:S(2)}, u32[]{:S(2)}) collective-permute-start(f32[256]{0:T(256)S(1)} %add.339), channel_id=1, source_target_pairs={{4,0},{8,4},{12,8},{16,12},{20,16},{24,20},{28,24},{5,1},{9,5},{13... | collective-permute-start | bytes 3080 | tf_op jit(solution)/shard_map/while/body/eval_jaxpr/ppermute | solution.py:12
  548.9 5.8 collective-permute-start.1
  555.0 5.8 collective-permute-start.1
  561.1 5.8 collective-permute-start.1
Sparse Core Ops, SparseCore 0:
  290.5 70.0 all-reduce.2
  579.1 35.6 all-gather.2
